TPU v7x, 32 devices: a whole 2x2x4 slice. The times are simulated.
32 devices in a mesh: row: 4 (over z), col: 8 (over y, x, core).
Axes of the slice: x: 2, y: 2, z: 4, core: 2. Of those that a mesh axis runs over, the one named last changes fastest.
Arguments:
- photo_features: bfloat16 [384, 1152], P(('row', 'col')), may hold values from -6 to 6
- sentence_features: bfloat16 [384, 1152], P(('row', 'col')), may hold values from -6 to 6
- described_photo_number: int32 [384], P(('row', 'col')), may hold values from 0 to 383, each once
- logit_multiplier: float32 [], replicated, may hold values from 3 to 8
- logit_offset: float32 [], replicated, may hold values from -4 to -1
Outputs:
- img_grad: float32 [384, 1152], P(('row', 'col'))
- txt_grad: float32 [384, 1152], P(('row', 'col'))
Inputs may be any that keep to these rules, and one draw needn't show every extreme that they name: `described_photo_number`: every image index appears exactly once among the text ids.
All inputs are finite; a program needn't handle non-finite values.
Results may differ from a plain program's by a relative error of at most 0.004.
Values may be sent and summed in bfloat16 or wider, within the bound.
A program may use at most 64 MiB of HBM per device.

v0:
```python
import functools

import jax
import jax.numpy as jnp
from jax import lax
from jax.experimental import pallas as pl
from jax.experimental.pallas import tpu as pltpu
from jax.sharding import PartitionSpec as P

MESH = pl.DeviceIdType.MESH
PAD, OWN, QUAD, LANES = 16, 12, 4, 128
F32 = jnp.float32
BF16 = jnp.bfloat16


def spots(main):
    return [
        (QUAD * q, LANES * h, LANES * (3 * h + q)) for h in range(2) for q in range(3)
    ]


def partner(me, step, count):
    if count & (count - 1):
        return lax.rem(me + step, count), lax.rem(me + count - step, count)
    bit = 1
    peer = me
    while bit <= step:
        if step & bit:
            peer = peer + bit * (1 - 2 * lax.rem(me // bit, 2))
        bit *= 2
    return peer, peer


def unit_rows(values):
    scale = lax.rsqrt(jnp.sum(values * values, axis=1, keepdims=True) + 1e-06)
    return values * scale, scale


def back_through(unit, scale, upstream):
    inner = jnp.sum(unit * upstream, axis=1, keepdims=True)
    return scale * (upstream - unit * inner)


def kernel(
    n_row, n_col,
    mul_ref, off_ref, ids_hbm, img_hbm, txt_hbm, img_grad, txt_grad,
    ids_ref, img_raw, txt_raw, img_unit, txt_unit,
    img_all, txt_all, img_tail, txt_tail, img_sum, txt_sum, img_part, txt_part, img_in, txt_in,
    load_sem, img_send, img_recv, txt_send, txt_recv, img_back, img_got, txt_back, txt_got,
):
    row, col = lax.axis_index("row"), lax.axis_index("col")
    loads = [
        pltpu.make_async_copy(txt_hbm, txt_raw, load_sem.at[0]),
        pltpu.make_async_copy(img_hbm, img_raw, load_sem.at[1]),
        pltpu.make_async_copy(ids_hbm, ids_ref, load_sem.at[2]),
    ]
    for load in loads:
        load.start()

    col_peer = [None] + [partner(col, d, n_col) for d in range(1, n_col)]
    row_peer = [None] + [partner(row, d, n_row) for d in range(1, n_row)]
    barrier = pltpu.get_barrier_semaphore()
    for d in range(1, n_col):
        pl.semaphore_signal(barrier, inc=1, device_id=(row, col_peer[d][1]), device_id_type=MESH)
    for d in range(1, n_row):
        pl.semaphore_signal(barrier, inc=1, device_id=(row_peer[d][1], col), device_id_type=MESH)

    width = img_raw.shape[1]
    main = img_all.shape[1]
    rest = width - main
    places = spots(main)

    place = lax.broadcasted_iota(jnp.int32, (n_col * PAD, 1), 0)
    slot, entry = place // PAD, lax.rem(place, PAD)
    owner = jnp.zeros((n_col * PAD, 1), jnp.int32) + col
    for d in range(1, n_col):
        owner = jnp.where(slot == d, col_peer[d][1], owner)
    img_ids = (row * n_col + owner) * OWN + entry
    at = lax.broadcasted_iota(jnp.int32, (1, n_row * PAD), 1)
    real = (entry < OWN) & (lax.rem(at, PAD) < OWN)
    zeros = jnp.zeros((PAD - OWN, rest), F32)
    for tail, count in ((img_tail, n_col), (txt_tail, n_row)):
        for d in range(count):
            tail[pl.ds(d * PAD + OWN, PAD - OWN)] = zeros

    loads[2].wait()
    lane = lax.rem(lax.broadcasted_iota(jnp.int32, (1, LANES), 1), PAD)
    numbers = jnp.zeros((1, LANES), jnp.int32)
    for t in range(OWN):
        numbers = jnp.where(lane == t, ids_ref[t], numbers)
    low = lax.rem(numbers, 256).astype(F32)
    high = (numbers // 256).astype(F32)

    def pack(raw, unit, whole, tail, packed):
        value, scale = unit_rows(raw[...].astype(F32))
        unit[...] = value
        tail[pl.ds(0, OWN)] = value[:, main:]
        packed[pl.ds(0, OWN)] = value[:, :main]
        for first, lanes, to in places:
            packed[pl.ds(OWN, QUAD), pl.ds(to, LANES)] = tail[
                pl.ds(first, QUAD), pl.ds(lanes, LANES)
            ]
        return scale

    free = pl.ds(main - LANES, LANES)
    loads[0].wait()
    txt_pack = txt_sum.at[pl.ds(0, PAD)]
    txt_scale = pack(txt_raw, txt_unit, txt_all, txt_tail, txt_pack)
    txt_pack[pl.ds(OWN, QUAD), free] = jnp.zeros((QUAD, LANES), F32)
    txt_pack[pl.ds(OWN, 1), free] = low
    txt_pack[pl.ds(OWN + 1, 1), free] = high
    txt_all[pl.ds(0, PAD)] = txt_pack[...].astype(BF16)
    pl.semaphore_wait(barrier, n_col + n_row - 2)

    def send(src, dst, d, sems, peer):
        return pltpu.make_async_remote_copy(
            src_ref=src, dst_ref=dst.at[pl.ds(d * PAD, PAD)],
            send_sem=sems[0].at[d], recv_sem=sems[1].at[d],
            device_id=peer, device_id_type=MESH,
        )

    txt_copies = [
        send(txt_all.at[pl.ds(0, PAD)], txt_all, d, (txt_send, txt_recv), (row_peer[d][0], col))
        for d in range(1, n_row)
    ]
    for copy in reversed(txt_copies):
        copy.start()
    loads[1].wait()
    img_pack = img_sum.at[pl.ds(0, PAD)]
    img_scale = pack(img_raw, img_unit, img_all, img_tail, img_pack)
    img_pack[pl.ds(OWN, QUAD), free] = jnp.zeros((QUAD, LANES), F32)
    img_all[pl.ds(0, PAD)] = img_pack[...].astype(BF16)
    img_copies = [
        send(img_all.at[pl.ds(0, PAD)], img_all, d, (img_send, img_recv), (row, col_peer[d][0]))
        for d in range(1, n_col)
    ]
    for copy in img_copies:
        copy.start()

    def unpack(whole, tail, d):
        block = whole[pl.ds(d * PAD, PAD), pl.ds(0, main - LANES)].astype(F32)
        for first, lanes, to in places:
            tail[pl.ds(d * PAD + first, QUAD), pl.ds(lanes, LANES)] = block[
                OWN:, to : to + LANES
            ]

    img_copies[0].wait_recv()
    unpack(img_all, img_tail, 1)
    for d, copy in enumerate(txt_copies, 1):
        copy.wait_recv()
        unpack(txt_all, txt_tail, d)
    digits = []
    for digit in range(2):
        line = jnp.zeros((1, n_row * PAD), F32)
        for d in range(n_row):
            block = txt_all[pl.ds(d * PAD, PAD), free].astype(F32)[OWN + digit : OWN + digit + 1]
            if n_row * PAD > LANES:
                block = jnp.concatenate([block] * (n_row * PAD // LANES), axis=1)
            line = jnp.where(at // PAD == d, block[:, : n_row * PAD], line)
        digits.append(line)
    txt_ids = (digits[0] + 256.0 * digits[1]).astype(jnp.int32)
    texts, text_tails = txt_all[...], txt_tail[...].astype(BF16)
    multiplier, offset = mul_ref[...], off_ref[...]
    across = (((1,), (1,)), ((), ()))
    down = (((0,), (0,)), ((), ()))

    def weigh(first, count):
        rows = pl.ds(first * PAD, count * PAD)
        logits = multiplier * (
            lax.dot_general(img_all[rows], texts, across, preferred_element_type=F32)
            + lax.dot_general(
                img_tail[rows].astype(BF16), text_tails, across, preferred_element_type=F32
            )
        ) + offset
        span = slice(first * PAD, (first + count) * PAD)
        match = img_ids[span] == txt_ids
        weights = jnp.where(match, -multiplier, multiplier) * jax.nn.sigmoid(
            jnp.where(match, -logits, logits)
        )
        return jnp.where(real[span], weights, 0.0).astype(BF16)

    def partial(head, tail, total, part, copies, start, count):
        total[pl.ds(start * PAD, count * PAD)] = head
        for d in reversed(range(count)):
            for first, lanes, to in places:
                total[pl.ds((start + d) * PAD + OWN, QUAD), pl.ds(to, LANES)] = tail[
                    d * PAD + first : d * PAD + first + QUAD, lanes : lanes + LANES
                ]
            if start + d:
                block = pl.ds((start + d) * PAD, PAD)
                part[block] = total[block].astype(BF16)
                copies[start + d - 1].start()

    img_backs = [
        send(img_part.at[pl.ds(d * PAD, PAD)], img_in, d, (img_back, img_got), (row, col_peer[d][1]))
        for d in range(1, n_col)
    ]
    txt_backs = [
        send(txt_part.at[pl.ds(d * PAD, PAD)], txt_in, d, (txt_back, txt_got), (row_peer[d][1], col))
        for d in range(1, n_row)
    ]

    def img_partial(weights, first, count):
        partial(
            jnp.dot(weights, texts, preferred_element_type=F32),
            jnp.dot(weights, text_tails, preferred_element_type=F32),
            img_sum, img_part, img_backs, first, count,
        )

    half = n_col // 2
    for d in range(2, half):
        img_copies[d - 1].wait_recv()
        unpack(img_all, img_tail, d)
    near = weigh(0, half)
    img_partial(near, 0, half)
    for d in range(half, n_col):
        img_copies[d - 1].wait_recv()
        unpack(img_all, img_tail, d)
    far = weigh(half, n_col - half)
    weights = jnp.concatenate([near, far], axis=0)
    partial(
        lax.dot_general(weights, img_all[...], down, preferred_element_type=F32),
        lax.dot_general(weights, img_tail[...].astype(BF16), down, preferred_element_type=F32),
        txt_sum, txt_part, txt_backs, 0, n_row,
    )
    img_partial(far, half, n_col - half)

    def finish(grad, total, copies, arrived, unit, scale):
        up = total[pl.ds(0, PAD)]
        for d, copy in enumerate(copies, 1):
            copy.wait_recv()
            up = up + arrived[pl.ds(d * PAD, PAD)].astype(F32)
        grad[:, pl.ds(0, main)] = up[:OWN]
        for first, lanes, to in places:
            grad[pl.ds(first, QUAD), pl.ds(main + lanes, LANES)] = up[OWN:, to : to + LANES]
        grad[...] = back_through(unit[...], scale, grad[...])

    finish(txt_grad, txt_sum, txt_backs, txt_in, txt_unit, txt_scale)
    finish(img_grad, img_sum, img_backs, img_in, img_unit, img_scale)
    for copy in txt_copies + img_copies + img_backs + txt_backs:
        copy.wait_send()


def store(img_ref, txt_ref, img_out, txt_out, sem):
    copies = [
        pltpu.make_async_copy(img_ref, img_out, sem.at[0]),
        pltpu.make_async_copy(txt_ref, txt_out, sem.at[1]),
    ]
    for copy in copies:
        copy.start()
    for copy in copies:
        copy.wait()


def solution(mesh):
    n_row, n_col = mesh.shape["row"], mesh.shape["col"]
    placed = (P(("row", "col"), None), P(("row", "col"), None), P(("row", "col")), P(), P())

    def shards(photo_features, sentence_features, described_photo_number, multiplier, offset):
        own, width = photo_features.shape
        assert own == OWN and width % LANES == 0
        main = width - 2 * LANES
        assert main == 7 * LANES
        smem = pl.BlockSpec(memory_space=pltpu.SMEM)
        hbm = pl.BlockSpec(memory_space=pltpu.HBM)
        vmem = pl.BlockSpec(memory_space=pltpu.VMEM)
        held = pltpu.VMEM((own, width), F32)
        dma = pltpu.SemaphoreType.DMA
        rows, cols = n_row * PAD, n_col * PAD
        grads = pl.pallas_call(
            functools.partial(kernel, n_row, n_col),
            out_shape=(held, held),
            in_specs=[smem, smem, hbm, hbm, hbm],
            out_specs=(vmem, vmem),
            scratch_shapes=[
                pltpu.SMEM((own,), jnp.int32),
                pltpu.VMEM((own, width), BF16),
                pltpu.VMEM((own, width), BF16),
                pltpu.VMEM((own, width), F32),
                pltpu.VMEM((own, width), F32),
                pltpu.VMEM((cols, main), BF16),
                pltpu.VMEM((rows, main), BF16),
                pltpu.VMEM((cols, width - main), F32),
                pltpu.VMEM((rows, width - main), F32),
                pltpu.VMEM((cols, main), F32),
                pltpu.VMEM((rows, main), F32),
                pltpu.VMEM((cols, main), BF16),
                pltpu.VMEM((rows, main), BF16),
                pltpu.VMEM((cols, main), BF16),
                pltpu.VMEM((rows, main), BF16),
                dma((3,)),
                dma((n_col,)), dma((n_col,)), dma((n_row,)), dma((n_row,)),
                dma((n_col,)), dma((n_col,)), dma((n_row,)), dma((n_row,)),
            ],
            compiler_params=pltpu.CompilerParams(
                collective_id=0, has_side_effects=True, vmem_limit_bytes=60 * 2**20
            ),
        )(multiplier, offset, described_photo_number, photo_features, sentence_features)
        grad = jax.ShapeDtypeStruct((own, width), F32)
        return pl.pallas_call(
            store,
            out_shape=(grad, grad),
            in_specs=[vmem, vmem],
            out_specs=(hbm, hbm),
            scratch_shapes=[dma((2,))],
            compiler_params=pltpu.CompilerParams(vmem_limit_bytes=2**20),
        )(*grads)

    return jax.shard_map(
        shards,
        mesh=mesh,
        in_specs=placed,
        out_specs=(P(("row", "col"), None), P(("row", "col"), None)),
        check_vma=False,
    )
```

profile of v0, /device:TPU:0, one launch (start us, length us, event | category | flops | bytes accessed | tf_op | source)
XLA Modules:
  0.0 18.2 jit_solution(8096751754012341362)
XLA Ops:
  1.9 15.5 %shard_map.68 = (f32[12,1152]{1,0:T(8,128)S(1)}, f32[12,1152]{1,0:T(8,128)S(1)}) custom-call(f32[]{:T(128)S(6)} %copy.7.mul_ref, f32[]{:T(128)S(6)} %copy.8.off_ref, s32[12]{0:T(128)} %ids_hbm.1, bf16[12,1152]{1,0:T(8,128)(2,1)} %img_hbm.1, bf16[12,1152]{1,0:T(8,128)(2,1)} %txt_hbm.1), custom_call_target="tpu_custom_call" | custom-call | tf_op jit(solution)/shard_map/pallas_call | solution.py:270
  17.5 0.7 %shard_map.69 = (f32[12,1152]{1,0:T(8,128)}, f32[12,1152]{1,0:T(8,128)}) custom-call(f32[12,1152]{1,0:T(8,128)S(1)} %get-tuple-element.4.img_ref, f32[12,1152]{1,0:T(8,128)S(1)} %get-tuple-element.5.txt_ref), custom_call_target="tpu_custom_call" | custom-call | tf_op jit(solution)/shard_map/pallas_call | solution.py:300
where the time goes:
time: 18.4 us; the launch traced here: 18.2 us
  Pallas kernels  16.2 us (88%)
  between operations  1.93 us (10%)
    pallas_call x1, Pallas kernels, shards(): pl.pallas_call(functools.partial(kernel, n_row, n_col), out_shape=(held,...  15.5 us
    pallas_call x1, Pallas kernels, shards(): pl.pallas_call(store, out_shape=(grad, grad), in_specs=[vmem, vmem], out_...  0.68 us

commit v1 on v0

--- a/solution.py
+++ b/solution.py
@@ -91,25 +91,25 @@
     low = lax.rem(numbers, 256).astype(F32)
     high = (numbers // 256).astype(F32)
 
-    def pack(raw, unit, whole, tail, packed):
-        value, scale = unit_rows(raw[...].astype(F32))
-        unit[...] = value
+    loads[0].wait()
+    loads[1].wait()
+    txt_value, txt_scale = unit_rows(txt_raw[...].astype(F32))
+    img_value, img_scale = unit_rows(img_raw[...].astype(F32))
+    txt_unit[...] = txt_value
+    img_unit[...] = img_value
+    free = pl.ds(main - LANES, LANES)
+    txt_sum[pl.ds(OWN, QUAD), free] = jnp.concatenate([low, high, low, high], axis=0)
+    img_sum[pl.ds(OWN, QUAD), free] = jnp.zeros((QUAD, LANES), F32)
+    for value, tail, packed in ((txt_value, txt_tail, txt_sum), (img_value, img_tail, img_sum)):
         tail[pl.ds(0, OWN)] = value[:, main:]
         packed[pl.ds(0, OWN)] = value[:, :main]
         for first, lanes, to in places:
-            packed[pl.ds(OWN, QUAD), pl.ds(to, LANES)] = tail[
-                pl.ds(first, QUAD), pl.ds(lanes, LANES)
+            packed[pl.ds(OWN, QUAD), pl.ds(to, LANES)] = value[
+                first : first + QUAD, main + lanes : main + lanes + LANES
             ]
-        return scale
-
-    free = pl.ds(main - LANES, LANES)
-    loads[0].wait()
-    txt_pack = txt_sum.at[pl.ds(0, PAD)]
-    txt_scale = pack(txt_raw, txt_unit, txt_all, txt_tail, txt_pack)
-    txt_pack[pl.ds(OWN, QUAD), free] = jnp.zeros((QUAD, LANES), F32)
-    txt_pack[pl.ds(OWN, 1), free] = low
-    txt_pack[pl.ds(OWN + 1, 1), free] = high
-    txt_all[pl.ds(0, PAD)] = txt_pack[...].astype(BF16)
+    txt_all[pl.ds(0, PAD)] = txt_sum[pl.ds(0, PAD)].astype(BF16)
+    img_all[pl.ds(0, PAD)] = img_sum[pl.ds(0, PAD)].astype(BF16)
+
     pl.semaphore_wait(barrier, n_col + n_row - 2)
 
     def send(src, dst, d, sems, peer):
@@ -123,18 +123,13 @@
         send(txt_all.at[pl.ds(0, PAD)], txt_all, d, (txt_send, txt_recv), (row_peer[d][0], col))
         for d in range(1, n_row)
     ]
-    for copy in reversed(txt_copies):
-        copy.start()
-    loads[1].wait()
-    img_pack = img_sum.at[pl.ds(0, PAD)]
-    img_scale = pack(img_raw, img_unit, img_all, img_tail, img_pack)
-    img_pack[pl.ds(OWN, QUAD), free] = jnp.zeros((QUAD, LANES), F32)
-    img_all[pl.ds(0, PAD)] = img_pack[...].astype(BF16)
     img_copies = [
         send(img_all.at[pl.ds(0, PAD)], img_all, d, (img_send, img_recv), (row, col_peer[d][0]))
         for d in range(1, n_col)
     ]
-    for copy in img_copies:
+    for copy in reversed(txt_copies):
+        copy.start()
+    for copy in reversed(img_copies):
         copy.start()
 
     def unpack(whole, tail, d):
@@ -207,23 +202,16 @@
             img_sum, img_part, img_backs, first, count,
         )
 
-    half = n_col // 2
-    for d in range(2, half):
+    for d in range(2, n_col):
         img_copies[d - 1].wait_recv()
         unpack(img_all, img_tail, d)
-    near = weigh(0, half)
-    img_partial(near, 0, half)
-    for d in range(half, n_col):
-        img_copies[d - 1].wait_recv()
-        unpack(img_all, img_tail, d)
-    far = weigh(half, n_col - half)
-    weights = jnp.concatenate([near, far], axis=0)
+    weights = weigh(0, n_col)
     partial(
         lax.dot_general(weights, img_all[...], down, preferred_element_type=F32),
         lax.dot_general(weights, img_tail[...].astype(BF16), down, preferred_element_type=F32),
         txt_sum, txt_part, txt_backs, 0, n_row,
     )
-    img_partial(far, half, n_col - half)
+    img_partial(weights, 0, n_col)
 
     def finish(grad, total, copies, arrived, unit, scale):
         up = total[pl.ds(0, PAD)]

time: 18.4 us -> 18.3 us (level)
  no operation moved by 1% of the time
where the time goes in v1:
time: 18.3 us; the launch traced here: 18.1 us
  Pallas kernels  16.2 us (89%)
  between operations  1.93 us (11%)
    pallas_call x1, Pallas kernels, shards(): pl.pallas_call(functools.partial(kernel, n_row, n_col), out_shape=(held,...  15.5 us
    pallas_call x1, Pallas kernels, shards(): pl.pallas_call(store, out_shape=(grad, grad), in_specs=[vmem, vmem], out_...  0.68 us

profile of v1, /device:TPU:0, one launch (start us, length us, event | category | flops | bytes accessed | tf_op | source)
XLA Modules:
  0.0 18.1 jit_solution(5020251683722793594)
XLA Ops:
  1.9 15.5 %shard_map.68 = (f32[12,1152]{1,0:T(8,128)S(1)}, f32[12,1152]{1,0:T(8,128)S(1)}) custom-call(f32[]{:T(128)S(6)} %copy.7.mul_ref, f32[]{:T(128)S(6)} %copy.8.off_ref, s32[12]{0:T(128)} %ids_hbm.1, bf16[12,1152]{1,0:T(8,128)(2,1)} %img_hbm.1, bf16[12,1152]{1,0:T(8,128)(2,1)} %txt_hbm.1), custom_call_target="tpu_custom_call" | custom-call | tf_op jit(solution)/shard_map/pallas_call | solution.py:258
  17.4 0.7 %shard_map.69 = (f32[12,1152]{1,0:T(8,128)}, f32[12,1152]{1,0:T(8,128)}) custom-call(f32[12,1152]{1,0:T(8,128)S(1)} %get-tuple-element.4.img_ref, f32[12,1152]{1,0:T(8,128)S(1)} %get-tuple-element.5.txt_ref), custom_call_target="tpu_custom_call" | custom-call | tf_op jit(solution)/shard_map/pallas_call | solution.py:288

commit v2 on v1

--- a/solution.py
+++ b/solution.py
@@ -20,8 +20,7 @@
 
 
 def partner(me, step, count):
-    if count & (count - 1):
-        return lax.rem(me + step, count), lax.rem(me + count - step, count)
+    assert count & (count - 1) == 0
     bit = 1
     peer = me
     while bit <= step:
@@ -45,8 +44,8 @@
     n_row, n_col,
     mul_ref, off_ref, ids_hbm, img_hbm, txt_hbm, img_grad, txt_grad,
     ids_ref, img_raw, txt_raw, img_unit, txt_unit,
-    img_all, txt_all, img_tail, txt_tail, img_sum, txt_sum, img_part, txt_part, img_in, txt_in,
-    load_sem, img_send, img_recv, txt_send, txt_recv, img_back, img_got, txt_back, txt_got,
+    img_all, txt_all, img_tail, txt_tail, img_sum, txt_sum, img_part, txt_part, img_in, txt_in, img_mid,
+    load_sem, mid_send, mid_recv, img_send, img_recv, txt_send, txt_recv, img_back, img_got, txt_back, txt_got,
 ):
     row, col = lax.axis_index("row"), lax.axis_index("col")
     loads = [
@@ -123,14 +122,20 @@
         send(txt_all.at[pl.ds(0, PAD)], txt_all, d, (txt_send, txt_recv), (row_peer[d][0], col))
         for d in range(1, n_row)
     ]
-    img_copies = [
-        send(img_all.at[pl.ds(0, PAD)], img_all, d, (img_send, img_recv), (row, col_peer[d][0]))
+    sibling = (row, col_peer[1][0])
+    img_copies = {
+        d: send(
+            img_all.at[pl.ds((d - 1) * PAD if d % 2 else 0, PAD)], img_all, d,
+            (img_send, img_recv), sibling if d % 2 else (row, col_peer[d][0]),
+        )
         for d in range(1, n_col)
-    ]
+    }
+    evens = list(range(2, n_col, 2))
     for copy in reversed(txt_copies):
         copy.start()
-    for copy in reversed(img_copies):
-        copy.start()
+    for d in reversed(evens):
+        img_copies[d].start()
+    img_copies[1].start()
 
     def unpack(whole, tail, d):
         block = whole[pl.ds(d * PAD, PAD), pl.ds(0, main - LANES)].astype(F32)
@@ -139,8 +144,13 @@
                 OWN:, to : to + LANES
             ]
 
-    img_copies[0].wait_recv()
-    unpack(img_all, img_tail, 1)
+    for d in evens:
+        img_copies[d].wait_recv()
+        img_copies[d + 1].start()
+    for d in [1] + evens:
+        if d == 1:
+            img_copies[d].wait_recv()
+        unpack(img_all, img_tail, d)
     for d, copy in enumerate(txt_copies, 1):
         copy.wait_recv()
         unpack(txt_all, txt_tail, d)
@@ -174,48 +184,60 @@
         )
         return jnp.where(real[span], weights, 0.0).astype(BF16)
 
-    def partial(head, tail, total, part, copies, start, count):
-        total[pl.ds(start * PAD, count * PAD)] = head
-        for d in reversed(range(count)):
-            for first, lanes, to in places:
-                total[pl.ds((start + d) * PAD + OWN, QUAD), pl.ds(to, LANES)] = tail[
-                    d * PAD + first : d * PAD + first + QUAD, lanes : lanes + LANES
-                ]
-            if start + d:
-                block = pl.ds((start + d) * PAD, PAD)
-                part[block] = total[block].astype(BF16)
-                copies[start + d - 1].start()
-
-    img_backs = [
-        send(img_part.at[pl.ds(d * PAD, PAD)], img_in, d, (img_back, img_got), (row, col_peer[d][1]))
-        for d in range(1, n_col)
-    ]
+    def spread(total, tail, d):
+        for first, lanes, to in places:
+            total[pl.ds(d * PAD + OWN, QUAD), pl.ds(to, LANES)] = tail[
+                d * PAD + first : d * PAD + first + QUAD, lanes : lanes + LANES
+            ]
+
+    for d in evens:
+        img_copies[d + 1].wait_recv()
+        unpack(img_all, img_tail, d + 1)
+    weights = weigh(0, n_col)
+
     txt_backs = [
         send(txt_part.at[pl.ds(d * PAD, PAD)], txt_in, d, (txt_back, txt_got), (row_peer[d][1], col))
         for d in range(1, n_row)
     ]
-
-    def img_partial(weights, first, count):
-        partial(
-            jnp.dot(weights, texts, preferred_element_type=F32),
-            jnp.dot(weights, text_tails, preferred_element_type=F32),
-            img_sum, img_part, img_backs, first, count,
+    txt_sum[...] = lax.dot_general(weights, img_all[...], down, preferred_element_type=F32)
+    tail = lax.dot_general(
+        weights, img_tail[...].astype(BF16), down, preferred_element_type=F32
+    )
+    for d in reversed(range(n_row)):
+        spread(txt_sum, tail, d)
+        if d:
+            block = pl.ds(d * PAD, PAD)
+            txt_part[block] = txt_sum[block].astype(BF16)
+            txt_backs[d - 1].start()
+
+    mids = {
+        d: send(img_part.at[pl.ds((d + 1) * PAD, PAD)], img_mid, d, (mid_send, mid_recv), sibling)
+        for d in evens
+    }
+    img_backs = {
+        d: send(
+            img_part.at[pl.ds(d * PAD, PAD)], img_in, d, (img_back, img_got), (row, col_peer[d][1])
         )
-
-    for d in range(2, n_col):
-        img_copies[d - 1].wait_recv()
-        unpack(img_all, img_tail, d)
-    weights = weigh(0, n_col)
-    partial(
-        lax.dot_general(weights, img_all[...], down, preferred_element_type=F32),
-        lax.dot_general(weights, img_tail[...].astype(BF16), down, preferred_element_type=F32),
-        txt_sum, txt_part, txt_backs, 0, n_row,
-    )
-    img_partial(weights, 0, n_col)
+        for d in [1] + evens
+    }
+    img_sum[...] = jnp.dot(weights, texts, preferred_element_type=F32)
+    tail = jnp.dot(weights, text_tails, preferred_element_type=F32)
+    for d in reversed(range(1, n_col, 2)):
+        spread(img_sum, tail, d)
+        block = pl.ds(d * PAD, PAD)
+        img_part[block] = img_sum[block].astype(BF16)
+        (mids[d - 1] if d > 1 else img_backs[1]).start()
+    for d in reversed(range(0, n_col, 2)):
+        spread(img_sum, tail, d)
+    for d in reversed(evens):
+        mids[d].wait_recv()
+        block = pl.ds(d * PAD, PAD)
+        img_part[block] = (img_sum[block] + img_mid[block].astype(F32)).astype(BF16)
+        img_backs[d].start()
 
     def finish(grad, total, copies, arrived, unit, scale):
         up = total[pl.ds(0, PAD)]
-        for d, copy in enumerate(copies, 1):
+        for d, copy in copies:
             copy.wait_recv()
             up = up + arrived[pl.ds(d * PAD, PAD)].astype(F32)
         grad[:, pl.ds(0, main)] = up[:OWN]
@@ -223,10 +245,13 @@
             grad[pl.ds(first, QUAD), pl.ds(main + lanes, LANES)] = up[OWN:, to : to + LANES]
         grad[...] = back_through(unit[...], scale, grad[...])
 
-    finish(txt_grad, txt_sum, txt_backs, txt_in, txt_unit, txt_scale)
-    finish(img_grad, img_sum, img_backs, img_in, img_unit, img_scale)
-    for copy in txt_copies + img_copies + img_backs + txt_backs:
+    finish(txt_grad, txt_sum, list(enumerate(txt_backs, 1)), txt_in, txt_unit, txt_scale)
+    finish(img_grad, img_sum, list(img_backs.items()), img_in, img_unit, img_scale)
+    for copy in txt_copies + txt_backs:
         copy.wait_send()
+    for group in (img_copies, mids, img_backs):
+        for copy in group.values():
+            copy.wait_send()
 
 
 def store(img_ref, txt_ref, img_out, txt_out, sem):
@@ -276,7 +301,8 @@
                 pltpu.VMEM((rows, main), BF16),
                 pltpu.VMEM((cols, main), BF16),
                 pltpu.VMEM((rows, main), BF16),
-                dma((3,)),
+                pltpu.VMEM((cols, main), BF16),
+                dma((3,)), dma((n_col,)), dma((n_col,)),
                 dma((n_col,)), dma((n_col,)), dma((n_row,)), dma((n_row,)),
                 dma((n_col,)), dma((n_col,)), dma((n_row,)), dma((n_row,)),
             ],

time: 18.3 us -> 18.7 us (1.022)
  Pallas kernels: 16.2 us -> 16.5 us
    pallas_call x1, Pallas kernels: 15.5 us -> 15.9 us  [shards(): pl.pallas_call(functools.partial(kernel, n_row, n_col), out_shape=(held,...]
where the time goes in v2:
time: 18.7 us; the launch traced here: 18.5 us
  Pallas kernels  16.5 us (88%)
  between operations  1.93 us (10%)
    pallas_call x1, Pallas kernels, shards(): pl.pallas_call(functools.partial(kernel, n_row, n_col), out_shape=(held,...  15.9 us
    pallas_call x1, Pallas kernels, shards(): pl.pallas_call(store, out_shape=(grad, grad), in_specs=[vmem, vmem], out_...  0.68 us

profile of v2, /device:TPU:0, one launch (start us, length us, event | category | flops | bytes accessed | tf_op | source)
XLA Modules:
  0.0 18.5 jit_solution(10704788278040127199)
XLA Ops:
  1.9 15.9 %shard_map.68 = (f32[12,1152]{1,0:T(8,128)S(1)}, f32[12,1152]{1,0:T(8,128)S(1)}) custom-call(f32[]{:T(128)S(6)} %copy.7.mul_ref, f32[]{:T(128)S(6)} %copy.8.off_ref, s32[12]{0:T(128)} %ids_hbm.1, bf16[12,1152]{1,0:T(8,128)(2,1)} %img_hbm.1, bf16[12,1152]{1,0:T(8,128)(2,1)} %txt_hbm.1), custom_call_target="tpu_custom_call" | custom-call | tf_op jit(solution)/shard_map/pallas_call | solution.py:283
  17.8 0.7 %shard_map.69 = (f32[12,1152]{1,0:T(8,128)}, f32[12,1152]{1,0:T(8,128)}) custom-call(f32[12,1152]{1,0:T(8,128)S(1)} %get-tuple-element.4.img_ref, f32[12,1152]{1,0:T(8,128)S(1)} %get-tuple-element.5.txt_ref), custom_call_target="tpu_custom_call" | custom-call | tf_op jit(solution)/shard_map/pallas_call | solution.py:314

commit v3 on v1

--- a/solution.py
+++ b/solution.py
@@ -91,26 +91,21 @@
     low = lax.rem(numbers, 256).astype(F32)
     high = (numbers // 256).astype(F32)
 
-    loads[0].wait()
-    loads[1].wait()
-    txt_value, txt_scale = unit_rows(txt_raw[...].astype(F32))
-    img_value, img_scale = unit_rows(img_raw[...].astype(F32))
-    txt_unit[...] = txt_value
-    img_unit[...] = img_value
     free = pl.ds(main - LANES, LANES)
+    img_sum[pl.ds(OWN, QUAD), free] = jnp.zeros((QUAD, LANES), F32)
     txt_sum[pl.ds(OWN, QUAD), free] = jnp.concatenate([low, high, low, high], axis=0)
-    img_sum[pl.ds(OWN, QUAD), free] = jnp.zeros((QUAD, LANES), F32)
-    for value, tail, packed in ((txt_value, txt_tail, txt_sum), (img_value, img_tail, img_sum)):
+
+    def pack(raw, unit, tail, packed, whole):
+        value, scale = unit_rows(raw[...].astype(F32))
+        unit[...] = value
         tail[pl.ds(0, OWN)] = value[:, main:]
         packed[pl.ds(0, OWN)] = value[:, :main]
         for first, lanes, to in places:
             packed[pl.ds(OWN, QUAD), pl.ds(to, LANES)] = value[
                 first : first + QUAD, main + lanes : main + lanes + LANES
             ]
-    txt_all[pl.ds(0, PAD)] = txt_sum[pl.ds(0, PAD)].astype(BF16)
-    img_all[pl.ds(0, PAD)] = img_sum[pl.ds(0, PAD)].astype(BF16)
-
-    pl.semaphore_wait(barrier, n_col + n_row - 2)
+        whole[pl.ds(0, PAD)] = packed[pl.ds(0, PAD)].astype(BF16)
+        return scale
 
     def send(src, dst, d, sems, peer):
         return pltpu.make_async_remote_copy(
@@ -127,8 +122,13 @@
         send(img_all.at[pl.ds(0, PAD)], img_all, d, (img_send, img_recv), (row, col_peer[d][0]))
         for d in range(1, n_col)
     ]
+    loads[0].wait()
+    txt_scale = pack(txt_raw, txt_unit, txt_tail, txt_sum, txt_all)
+    pl.semaphore_wait(barrier, n_col + n_row - 2)
     for copy in reversed(txt_copies):
         copy.start()
+    loads[1].wait()
+    img_scale = pack(img_raw, img_unit, img_tail, img_sum, img_all)
     for copy in reversed(img_copies):
         copy.start()
 
@@ -139,8 +139,9 @@
                 OWN:, to : to + LANES
             ]
 
-    img_copies[0].wait_recv()
-    unpack(img_all, img_tail, 1)
+    for d, copy in enumerate(img_copies, 1):
+        copy.wait_recv()
+        unpack(img_all, img_tail, d)
     for d, copy in enumerate(txt_copies, 1):
         copy.wait_recv()
         unpack(txt_all, txt_tail, d)
@@ -202,9 +203,6 @@
             img_sum, img_part, img_backs, first, count,
         )
 
-    for d in range(2, n_col):
-        img_copies[d - 1].wait_recv()
-        unpack(img_all, img_tail, d)
     weights = weigh(0, n_col)
     partial(
         lax.dot_general(weights, img_all[...], down, preferred_element_type=F32),
@@ -223,8 +221,8 @@
             grad[pl.ds(first, QUAD), pl.ds(main + lanes, LANES)] = up[OWN:, to : to + LANES]
         grad[...] = back_through(unit[...], scale, grad[...])
 
+    finish(img_grad, img_sum, img_backs, img_in, img_unit, img_scale)
     finish(txt_grad, txt_sum, txt_backs, txt_in, txt_unit, txt_scale)
-    finish(img_grad, img_sum, img_backs, img_in, img_unit, img_scale)
     for copy in txt_copies + img_copies + img_backs + txt_backs:
         copy.wait_send()
 

time: 18.3 us -> 18.3 us (level)
  no operation moved by 1% of the time
where the time goes in v3:
time: 18.3 us; the launch traced here: 18.1 us
  Pallas kernels  16.1 us (88%)
  between operations  1.93 us (11%)
    pallas_call x1, Pallas kernels, shards(): pl.pallas_call(functools.partial(kernel, n_row, n_col), out_shape=(held,...  15.5 us
    pallas_call x1, Pallas kernels, shards(): pl.pallas_call(store, out_shape=(grad, grad), in_specs=[vmem, vmem], out_...  0.68 us

profile of v3, /device:TPU:0, one launch (start us, length us, event | category | flops | bytes accessed | tf_op | source)
XLA Modules:
  0.0 18.1 jit_solution(11524040975460550121)
XLA Ops:
  1.9 15.5 %shard_map.68 = (f32[12,1152]{1,0:T(8,128)S(1)}, f32[12,1152]{1,0:T(8,128)S(1)}) custom-call(f32[]{:T(128)S(6)} %copy.7.mul_ref, f32[]{:T(128)S(6)} %copy.8.off_ref, s32[12]{0:T(128)} %ids_hbm.1, bf16[12,1152]{1,0:T(8,128)(2,1)} %img_hbm.1, bf16[12,1152]{1,0:T(8,128)(2,1)} %txt_hbm.1), custom_call_target="tpu_custom_call" | custom-call | tf_op jit(solution)/shard_map/pallas_call | solution.py:256
  17.4 0.7 %shard_map.69 = (f32[12,1152]{1,0:T(8,128)}, f32[12,1152]{1,0:T(8,128)}) custom-call(f32[12,1152]{1,0:T(8,128)S(1)} %get-tuple-element.4.img_ref, f32[12,1152]{1,0:T(8,128)S(1)} %get-tuple-element.5.txt_ref), custom_call_target="tpu_custom_call" | custom-call | tf_op jit(solution)/shard_map/pallas_call | solution.py:286
